TPU v7x, 256 devices: a whole 4x4x8 slice. The times are simulated.
256 devices in a mesh: ops: 32 (over y, x, core), sec: 8 (over z).
Axes of the slice: x: 4, y: 4, z: 8, core: 2. Of those that a mesh axis runs over, the one named last changes fastest.
Arguments:
- left_ops: bfloat16 [128, 16, 256, 256], P('ops', 'sec'), as said below
- right_ops: bfloat16 [128, 16, 256, 256], P('ops', 'sec'), as said below
- pattern: int32 [128, 16], P('ops', 'sec'), may hold values from 0 to 1, as said below
- guess_vector: float32 [16, 256, 256], P('sec'), may hold values from -6 to 6
- precond: float32 [16, 256, 256], P('sec'), may hold values from 0.5 to 8
- rotation: bfloat16 [16, 256, 256], P('sec', None, 'ops'), may hold values from -1.5 to 1.5
Outputs:
- new_state: float32 [16, 256, 256], P('sec', 'ops')
- energy: float32 [1], replicated
- renormalized: bfloat16 [128, 16, 256, 256], P('ops', 'sec')
Inputs may be any that keep to these rules, and one draw needn't show every extreme that they name: pattern[k, s] is 1 where operator k has a block in sector s, else 0. Every block left_ops[k, s] is symmetric. Every block right_ops[k, s] is symmetric.
All inputs are finite; a program needn't handle non-finite values.
Results may differ from a plain program's by a relative error of at most 0.009.
Values may be sent and summed in bfloat16 or wider, within the bound.
No kernel may reach another device: no remote copies, remote signals or barrier semaphores. Data moves between devices by JAX's collectives and lax.ppermute only.
A program may use at most 64 MiB of HBM per device.

v0:
```python
import jax
import jax.numpy as jnp
from jax import lax
from jax.sharding import PartitionSpec as P


def local_sigma(vector, left_ops, right_ops, pattern):
    vec_low = vector.astype(jnp.bfloat16)
    halfway = jnp.einsum(
        "ksij,sjl->ksil", left_ops, vec_low, preferred_element_type=jnp.float32
    ).astype(jnp.bfloat16)
    halfway = halfway * pattern.astype(jnp.bfloat16)[:, :, None, None]
    return jnp.einsum("ksil,ksml->sim", halfway, right_ops, preferred_element_type=jnp.float32)


def local(left_ops, right_ops, pattern, guess_vector, precond, rotation):
    sector_count = guess_vector.shape[0]
    states = guess_vector.shape[1]
    row_count = states // lax.axis_size("ops")
    row_start = lax.axis_index("ops") * row_count
    entries = float(sector_count * lax.axis_size("sec") * states * states)

    def owned(array):
        return lax.dynamic_slice_in_dim(array, row_start, row_count, 1)

    rotate_full = lax.all_gather(rotation, "ops", axis=2, tiled=True)
    rotated = jnp.einsum(
        "ksij,sjl->ksil", left_ops, rotate_full, preferred_element_type=jnp.float32
    ).astype(jnp.bfloat16)
    renormalized = jnp.einsum(
        "sji,ksjl->ksil", rotate_full, rotated, preferred_element_type=jnp.float32
    ).astype(jnp.bfloat16)
    guess_rows = owned(guess_vector)
    guess_sum = lax.psum(jnp.sum(guess_rows * guess_rows), ("ops", "sec"))
    first_full = guess_vector * (1.0 / jnp.sqrt(guess_sum / entries + 1e-06))

    def apply_whole(vector):
        return lax.psum(local_sigma(vector, left_ops, right_ops, pattern), "ops")

    def local_part(array):
        return owned(array)

    def local_product(left, right):
        return jnp.sum(local_part(left) * local_part(right))

    image_first = apply_whole(first_full)
    rayleigh_first = lax.psum(local_product(first_full, image_first), ("ops", "sec")) / entries
    correction = (image_first - rayleigh_first * first_full) / precond
    correlation = lax.psum(local_product(first_full, correction), ("ops", "sec")) / entries
    orthogonal = correction - correlation * first_full
    orth_square = lax.psum(local_product(orthogonal, orthogonal), ("ops", "sec")) / entries
    second = orthogonal * (1.0 / jnp.sqrt(orth_square + 1e-06))
    image_second = apply_whole(second)
    coupling_sum, second_sum = lax.psum(
        (local_product(first_full, image_second), local_product(second, image_second)),
        ("ops", "sec"),
    )
    coupling = coupling_sum / entries
    rayleigh_second = second_sum / entries
    half_gap = (rayleigh_first - rayleigh_second) / 2
    energy = (rayleigh_first + rayleigh_second) / 2 - jnp.sqrt(
        half_gap * half_gap + coupling * coupling
    )
    weight_first = rayleigh_second - energy
    weight_second = -coupling
    scaling = jnp.sqrt(weight_first * weight_first + weight_second * weight_second)
    combined = (weight_first * first_full + weight_second * second) / scaling
    new_state = local_part(combined)
    return (new_state, jnp.reshape(energy, (1,)), renormalized)


def solution(mesh):
    return jax.shard_map(
        local,
        mesh=mesh,
        in_specs=(
            P("ops", "sec", None, None),
            P("ops", "sec", None, None),
            P("ops", "sec"),
            P("sec", None, None),
            P("sec", None, None),
            P("sec", None, "ops"),
        ),
        out_specs=(P("sec", "ops", None), P(), P("ops", "sec", None, None)),
        check_vma=False,
    )
```

profile of v0, /device:TPU:1, one launch (start us, length us, event | category | flops | bytes accessed | tf_op | source)
XLA Modules:
  0.0 659.4 jit_solution(3782549998908427796)
XLA Ops:
  7.2 0.0 all-reduce.4.cloned.1.call-start
  7.2 1.4 multiply_reduce_fusion.5
  8.6 81.4 %psum.56 = f32[]{:T(128)} all-reduce(f32[]{:T(128)} %multiply_reduce_fusion.5), channel_id=1, replica_groups=mesh['ops'=32,'sec'=8] {'ops','sec'}, use_global_device_ids=true, to_apply=%region_1.0 | all-reduce | flops 1 | bytes 8 | tf_op jit(solution)/shard_map/psum | solution.py:34
  90.7 1.1 broadcast_multiply_fusion.1
  91.9 2.8 fusion.8
  94.7 0.0 all-reduce.4.cloned.1.call-update
  94.7 0.0 all-reduce.6.cloned.1.call-start
  94.8 108.9 %all-reduce.4.cloned.1.call-done = f32[2,256,256]{2,1,0:T(8,128)} async-done(((f32[2,256,256]{2,1,0:T(8,128)}), f32[2,256,256]{2,1,0:T(8,128)}) %all-reduce.4.cloned.1.call-update) | async-done | bytes 524304 | tf_op jit(solution)/shard_map/psum | solution.py:38
  203.6 1.3 multiply_reduce_fusion.4
  205.0 76.8 %psum.58 = f32[]{:T(128)} all-reduce(f32[]{:T(128)} %multiply_reduce_fusion.4), channel_id=1, replica_groups=mesh['ops'=32,'sec'=8] {'ops','sec'}, use_global_device_ids=true, to_apply=%region_4.0 | all-reduce | flops 1 | bytes 8 | tf_op jit(solution)/shard_map/psum | solution.py:47
  282.5 1.1 subtract_divide_fusion
  283.6 0.6 multiply_reduce_fusion.3
  284.2 73.4 %psum.59 = f32[]{:T(128)} all-reduce(f32[]{:T(128)} %multiply_reduce_fusion.3), channel_id=1, replica_groups=mesh['ops'=32,'sec'=8] {'ops','sec'}, use_global_device_ids=true, to_apply=%region_6.0 | all-reduce | flops 1 | bytes 8 | tf_op jit(solution)/shard_map/psum | solution.py:49
  358.3 0.1 multiply_subtract_fusion
  358.5 0.6 multiply_reduce_fusion.2
  359.1 24.0 %all_gather.3 = bf16[2,256,256]{1,2,0:T(8,128)(2,1)S(1)} all-gather(bf16[2,256,8]{1,2,0:T(8,128)(2,1)S(1)} %copy-done.3), channel_id=1, replica_groups=mesh['ops'=32,'sec'=8] {'ops'}, dimensions={2}, use_global_device_ids=true | all-gather | bytes 270336 | tf_op jit(solution)/shard_map/all_gather | solution.py:26
  383.0 73.3 %psum.60 = f32[]{:T(128)} all-reduce(f32[]{:T(128)} %multiply_reduce_fusion.2), channel_id=1, replica_groups=mesh['ops'=32,'sec'=8] {'ops','sec'}, use_global_device_ids=true, to_apply=%region_8.0 | all-reduce | flops 1 | bytes 8 | tf_op jit(solution)/shard_map/psum | solution.py:51
  457.1 2.8 fusion.9
  459.9 0.7 fusion.3
  460.6 1.3 copy.11
  461.9 108.0 %all-reduce.6.cloned.1.call-done = f32[2,256,256]{2,1,0:T(8,128)} async-done(((f32[2,256,256]{2,1,0:T(8,128)}), f32[2,256,256]{2,1,0:T(8,128)}) %all-reduce.6.cloned.1.call-update) | async-done | bytes 524304 | tf_op jit(solution)/shard_map/psum | solution.py:38
  569.9 1.3 multiply_reduce_fusion
  571.2 76.9 %all-reduce = (f32[]{:T(128)}, f32[]{:T(128)}) all-reduce(f32[]{:T(128)} %get-tuple-element.7, f32[]{:T(128)} %get-tuple-element.6), channel_id=1, replica_groups=mesh['ops'=32,'sec'=8] {'ops','sec'}, use_global_device_ids=true, to_apply=%region_11.0 | all-reduce | flops 2 | bytes 16 | tf_op jit(solution)/shard_map/psum | solution.py:54
  650.8 0.6 add_divide_fusion
  (13 shorter events, 0.1 us)
Async XLA Ops:
  7.2 84.7 %copy-start = (bf16[4,2,256,256]{3,2,1,0:T(8,128)(2,1)S(1)}, bf16[4,2,256,256]{3,2,1,0:T(8,128)(2,1)}, u32[]{:S(2)}) copy-start(bf16[4,2,256,256]{3,2,1,0:T(8,128)(2,1)} %param.6) | copy-start | bytes 3145732
  7.2 84.6 %copy-start.4 = (s32[4,2]{0,1:T(2,128)S(1)}, s32[4,2]{0,1:T(2,128)}, u32[]{:S(2)}) copy-start(s32[4,2]{0,1:T(2,128)} %param.8) | copy-start | bytes 100
  7.2 196.4 %all-reduce.4.cloned.1.call-start = ((), (), s32[]{:S(2)}) async-start(), calls=%async_computation | async-start | bytes 1048576 | tf_op jit(solution)/shard_map/psum | solution.py:38
  91.8 190.6 %copy-start.1 = (f32[2,256,256]{2,1,0:T(8,128)S(1)}, f32[2,256,256]{2,1,0:T(8,128)}, u32[]{:S(2)}) copy-start(f32[2,256,256]{2,1,0:T(8,128)} %param.9) | copy-start | bytes 1572868
  91.8 190.6 %copy-start.2 = (f32[2,256,256]{2,1,0:T(8,128)S(1)}, f32[2,256,256]{2,1,0:T(8,128)}, u32[]{:S(2)}) copy-start(f32[2,256,256]{2,1,0:T(8,128)} %param.10) | copy-start | bytes 1572868
  94.7 475.2 %all-reduce.6.cloned.1.call-start = ((), (), s32[]{:S(2)}) async-start(), calls=%async_computation.1 | async-start | bytes 1048576 | tf_op jit(solution)/shard_map/psum | solution.py:38
  283.6 75.4 %copy-start.3 = (bf16[2,256,8]{1,2,0:T(8,128)(2,1)S(1)}, bf16[2,256,8]{1,2,0:T(8,128)(2,1)}, u32[]{:S(2)}) copy-start(bf16[2,256,8]{1,2,0:T(8,128)(2,1)} %param.11) | copy-start | bytes 24580
Sparse Core Ops, SparseCore 0:
  94.8 108.7 all-reduce.3
  460.0 109.8 all-reduce.5
where the time goes:
time: 661 us; the launch traced here: 659 us
  blocking collectives  406 us (61%)
  waiting for transfers between devices  217 us (33%)
  between operations  20.7 us (3%)
  other arithmetic  8.28 us (1%)
    psum x2, waiting for transfers between devices, apply_whole(): return lax.psum(local_sigma(vector, left_ops, right_ops, pattern), 'ops')  217 us
    psum x1, blocking collectives, local(): guess_sum = lax.psum(jnp.sum(guess_rows * guess_rows), ('ops', 'sec'))  81.4 us
    psum x1, blocking collectives, local(): lax.psum((local_product(first_full, image_second), local_product(second,...  76.9 us
    psum x1, blocking collectives, local(): lax.psum(local_product(first_full, image_first), ('ops', 'sec')) / entries  76.8 us
    psum x1, blocking collectives, local(): lax.psum(local_product(first_full, correction), ('ops', 'sec')) / entries  73.4 us
    psum x1, blocking collectives, local(): lax.psum(local_product(orthogonal, orthogonal), ('ops', 'sec')) / entries  73.3 us
    all_gather x1, blocking collectives, local(): rotate_full = lax.all_gather(rotation, 'ops', axis=2, tiled=True)  24 us
  transfers between devices with their start and end apart: 2, of which 2 were waited for; matrix products, arithmetic and copies ran while one was open for 0% of the time, Pallas kernels for 0%

commit v1 on v0

--- a/solution.py
+++ b/solution.py
@@ -44,7 +44,15 @@
         return jnp.sum(local_part(left) * local_part(right))
 
     image_first = apply_whole(first_full)
-    rayleigh_first = lax.psum(local_product(first_full, image_first), ("ops", "sec")) / entries
+
+    def _spread_inputs(a0, mesh_ax, device_axis):
+        for num in (mesh_ax, device_axis):
+            a0 = jax.lax.psum(a0, num)
+        return a0
+
+    rayleigh_first = (
+        _spread_inputs(local_product(first_full, image_first), "sec", device_axis="ops") / entries
+    )
     correction = (image_first - rayleigh_first * first_full) / precond
     correlation = lax.psum(local_product(first_full, correction), ("ops", "sec")) / entries
     orthogonal = correction - correlation * first_full

time: 661 us -> 664 us (level)
    psum x1 -> x2, blocking collectives: 76.8 us -> 81.5 us  [_spread_inputs(): a0 = jax.lax.psum(a0, num)]
where the time goes in v1:
time: 664 us; the launch traced here: 663 us
  blocking collectives  410 us (62%)
  waiting for transfers between devices  216 us (33%)
  between operations  20.7 us (3%)
  other arithmetic  8.28 us (1%)
    psum x2, waiting for transfers between devices, apply_whole(): return lax.psum(local_sigma(vector, left_ops, right_ops, pattern), 'ops')  216 us
    psum x2, blocking collectives, _spread_inputs(): a0 = jax.lax.psum(a0, num)  81.5 us
    psum x1, blocking collectives, local(): guess_sum = lax.psum(jnp.sum(guess_rows * guess_rows), ('ops', 'sec'))  81.4 us
    psum x1, blocking collectives, local(): lax.psum((local_product(first_full, image_second), local_product(second,...  76.9 us
    psum x1, blocking collectives, local(): lax.psum(local_product(orthogonal, orthogonal), ('ops', 'sec')) / entries  74.1 us
    psum x1, blocking collectives, local(): lax.psum(local_product(first_full, correction), ('ops', 'sec')) / entries  72.6 us
    all_gather x1, blocking collectives, local(): rotate_full = lax.all_gather(rotation, 'ops', axis=2, tiled=True)  23.4 us
  transfers between devices with their start and end apart: 2, of which 2 were waited for; matrix products, arithmetic and copies ran while one was open for 0% of the time, Pallas kernels for 0%

profile of v1, /device:TPU:1, one launch (start us, length us, event | category | flops | bytes accessed | tf_op | source)
XLA Modules:
  0.0 662.7 jit_solution(16715909615999951596)
XLA Ops:
  7.2 0.0 all-reduce.4.cloned.1.call-start
  7.2 1.4 multiply_reduce_fusion.5
  8.6 81.4 %psum.63 = f32[]{:T(128)} all-reduce(f32[]{:T(128)} %multiply_reduce_fusion.5), channel_id=1, replica_groups=mesh['ops'=32,'sec'=8] {'ops','sec'}, use_global_device_ids=true, to_apply=%region_1.0 | all-reduce | flops 1 | bytes 8 | tf_op jit(solution)/shard_map/psum | solution.py:34
  90.7 1.1 broadcast_multiply_fusion.1
  91.9 2.8 fusion.8
  94.7 0.0 all-reduce.6.cloned.1.call-start
  94.8 108.9 %all-reduce.4.cloned.1.call-done = f32[2,256,256]{2,1,0:T(8,128)} async-done(((f32[2,256,256]{2,1,0:T(8,128)}), f32[2,256,256]{2,1,0:T(8,128)}) %all-reduce.4.cloned.1.call-update) | async-done | bytes 524304 | tf_op jit(solution)/shard_map/psum | solution.py:38
  203.6 1.3 multiply_reduce_fusion.4
  205.0 14.3 %psum.65 = f32[]{:T(128)} all-reduce(f32[]{:T(128)} %multiply_reduce_fusion.4), channel_id=1, replica_groups=mesh['ops'=32,'sec'=8] {'sec'}, use_global_device_ids=true, to_apply=%region_4.0 | all-reduce | flops 1 | bytes 8 | tf_op jit(solution)/shard_map/psum | solution.py:50
  219.3 67.2 %psum.66 = f32[]{:T(128)} all-reduce(f32[]{:T(128)} %psum.65), channel_id=1, replica_groups=mesh['ops'=32,'sec'=8] {'ops'}, use_global_device_ids=true, to_apply=%region_5.0 | all-reduce | flops 1 | bytes 8 | tf_op jit(solution)/shard_map/psum | solution.py:50
  287.1 1.1 subtract_divide_fusion
  288.3 0.6 multiply_reduce_fusion.3
  288.9 72.6 %psum.67 = f32[]{:T(128)} all-reduce(f32[]{:T(128)} %multiply_reduce_fusion.3), channel_id=1, replica_groups=mesh['ops'=32,'sec'=8] {'ops','sec'}, use_global_device_ids=true, to_apply=%region_7.0 | all-reduce | flops 1 | bytes 8 | tf_op jit(solution)/shard_map/psum | solution.py:57
  362.2 0.1 multiply_subtract_fusion
  362.3 0.6 multiply_reduce_fusion.2
  362.9 23.4 %all_gather.3 = bf16[2,256,256]{1,2,0:T(8,128)(2,1)S(1)} all-gather(bf16[2,256,8]{1,2,0:T(8,128)(2,1)S(1)} %copy-done.3), channel_id=1, replica_groups=mesh['ops'=32,'sec'=8] {'ops'}, dimensions={2}, use_global_device_ids=true | all-gather | bytes 270336 | tf_op jit(solution)/shard_map/all_gather | solution.py:26
  386.2 74.1 %psum.68 = f32[]{:T(128)} all-reduce(f32[]{:T(128)} %multiply_reduce_fusion.2), channel_id=1, replica_groups=mesh['ops'=32,'sec'=8] {'ops','sec'}, use_global_device_ids=true, to_apply=%region_9.0 | all-reduce | flops 1 | bytes 8 | tf_op jit(solution)/shard_map/psum | solution.py:59
  461.1 2.8 fusion.9
  463.9 0.7 fusion.3
  464.7 1.3 copy.11
  466.0 107.2 %all-reduce.6.cloned.1.call-done = f32[2,256,256]{2,1,0:T(8,128)} async-done(((f32[2,256,256]{2,1,0:T(8,128)}), f32[2,256,256]{2,1,0:T(8,128)}) %all-reduce.6.cloned.1.call-update) | async-done | bytes 524304 | tf_op jit(solution)/shard_map/psum | solution.py:38
  573.2 1.3 multiply_reduce_fusion
  574.5 76.9 %all-reduce = (f32[]{:T(128)}, f32[]{:T(128)}) all-reduce(f32[]{:T(128)} %get-tuple-element.7, f32[]{:T(128)} %get-tuple-element.6), channel_id=1, replica_groups=mesh['ops'=32,'sec'=8] {'ops','sec'}, use_global_device_ids=true, to_apply=%region_12.0 | all-reduce | flops 2 | bytes 16 | tf_op jit(solution)/shard_map/psum | solution.py:62
  654.1 0.6 add_divide_fusion
  (14 shorter events, 0.1 us)
Async XLA Ops:
  7.2 84.7 %copy-start = (bf16[4,2,256,256]{3,2,1,0:T(8,128)(2,1)S(1)}, bf16[4,2,256,256]{3,2,1,0:T(8,128)(2,1)}, u32[]{:S(2)}) copy-start(bf16[4,2,256,256]{3,2,1,0:T(8,128)(2,1)} %param.6) | copy-start | bytes 3145732
  7.2 84.6 %copy-start.4 = (s32[4,2]{0,1:T(2,128)S(1)}, s32[4,2]{0,1:T(2,128)}, u32[]{:S(2)}) copy-start(s32[4,2]{0,1:T(2,128)} %param.8) | copy-start | bytes 100
  7.2 196.4 %all-reduce.4.cloned.1.call-start = ((), (), s32[]{:S(2)}) async-start(), calls=%async_computation | async-start | bytes 1048576 | tf_op jit(solution)/shard_map/psum | solution.py:38
  91.8 195.3 %copy-start.1 = (f32[2,256,256]{2,1,0:T(8,128)S(1)}, f32[2,256,256]{2,1,0:T(8,128)}, u32[]{:S(2)}) copy-start(f32[2,256,256]{2,1,0:T(8,128)} %param.9) | copy-start | bytes 1572868
  91.8 195.3 %copy-start.2 = (f32[2,256,256]{2,1,0:T(8,128)S(1)}, f32[2,256,256]{2,1,0:T(8,128)}, u32[]{:S(2)}) copy-start(f32[2,256,256]{2,1,0:T(8,128)} %param.10) | copy-start | bytes 1572868
  94.7 478.5 %all-reduce.6.cloned.1.call-start = ((), (), s32[]{:S(2)}) async-start(), calls=%async_computation.1 | async-start | bytes 1048576 | tf_op jit(solution)/shard_map/psum | solution.py:38
  288.3 74.6 %copy-start.3 = (bf16[2,256,8]{1,2,0:T(8,128)(2,1)S(1)}, bf16[2,256,8]{1,2,0:T(8,128)(2,1)}, u32[]{:S(2)}) copy-start(bf16[2,256,8]{1,2,0:T(8,128)(2,1)} %param.11) | copy-start | bytes 24580
Sparse Core Ops, SparseCore 0:
  94.8 108.7 all-reduce.3
  464.0 109.0 all-reduce.5
